TPU v7x, 32 devices: a whole 2x2x4 slice. The times are simulated.
32 devices in a mesh: dp: 16 (over z, x, core), tensor: 2 (over y).
Axes of the slice: x: 2, y: 2, z: 4, core: 2. Of those that a mesh axis runs over, the one named last changes fastest.
Arguments:
- tokens: bfloat16 [16384, 1024], P(('dp', 'tensor')), may hold values from -6 to 6
- cotangent: bfloat16 [16384, 1024], P(('dp', 'tensor')), may hold values from -6 to 6
- sequence_lengths: int32 [64], replicated, may hold values from 0 to 1024, as said below
- sequence_group: int32 [64], replicated, may hold values from 0 to 15
- sequence_offset: int32 [64], replicated, may hold values from 0 to 15, as said below
- mixer_gain: bfloat16 [1024], replicated, may hold values from 0.5 to 1.5
- query_weight: bfloat16 [1024, 512], P('dp', 'tensor'), may hold values from -0.1875 to 0.1875
- key_weight: bfloat16 [1024, 512], P('dp', 'tensor'), may hold values from -0.1875 to 0.1875
- value_weight: bfloat16 [1024, 1024], P('dp', 'tensor'), may hold values from -0.1875 to 0.1875
- output_gate: bfloat16 [1024, 1024], P('dp', 'tensor'), may hold values from -0.1875 to 0.1875
- output_weight: bfloat16 [1024, 1024], P('dp', 'tensor'), may hold values from -0.375 to 0.375
- decay_down: bfloat16 [1024, 16], replicated, may hold values from -0.1875 to 0.1875
- decay_up: bfloat16 [16, 512], replicated, may hold values from -1.5 to 1.5
- decay_bias: bfloat16 [512], replicated, may hold values from -2 to 6
- head_gain: bfloat16 [256], replicated, may hold values from 0.5 to 1.5
- feed_gain: bfloat16 [1024], replicated, may hold values from 0.5 to 1.5
- feed_gate: bfloat16 [1024, 2816], P('dp', 'tensor'), may hold values from -0.1875 to 0.1875
- feed_up: bfloat16 [1024, 2816], P('dp', 'tensor'), may hold values from -0.1875 to 0.1875
- feed_down: bfloat16 [1024, 2816], P('dp', 'tensor'), may hold values from -0.15625 to 0.15625
Outputs:
- output: bfloat16 [16384, 1024], P(('dp', 'tensor'))
- input_grad: float32 [16384, 1024], P(('dp', 'tensor'))
- mixer_gain_grad: float32 [1024], replicated
- query_weight_grad: float32 [1024, 512], P('dp', 'tensor')
- key_weight_grad: float32 [1024, 512], P('dp', 'tensor')
- value_weight_grad: float32 [1024, 1024], P('dp', 'tensor')
- output_gate_grad: float32 [1024, 1024], P('dp', 'tensor')
- output_weight_grad: float32 [1024, 1024], P('dp', 'tensor')
- decay_down_grad: float32 [1024, 16], replicated
- decay_up_grad: float32 [16, 512], replicated
- decay_bias_grad: float32 [512], replicated
- head_gain_grad: float32 [256], replicated
- feed_gain_grad: float32 [1024], replicated
- feed_gate_grad: float32 [1024, 2816], P('dp', 'tensor')
- feed_up_grad: float32 [1024, 2816], P('dp', 'tensor')
- feed_down_grad: float32 [1024, 2816], P('dp', 'tensor')
Inputs may be any that keep to these rules, and one draw needn't show every extreme that they name: Record i is one sequence of sequence_lengths[i] tokens, held by index sequence_group[i] along dp and starting at span sequence_offset[i] of 64 tokens within that index's 1024 slots; a length of 0 marks an unused record. Each index along dp has 4 records and at least one live sequence; its live sequences, each rounded up to whole spans, are disjoint and lie within its 1024 slots, and one of them starts at span 0. Some index holds a single sequence of 1024 tokens. `sequence_offset`: an unused record has offset 0. Some index has a sequence that starts at its last span.
All inputs are finite; a program needn't handle non-finite values.
Results may differ from a plain program's by a relative error of at most 0.015.
Values may be sent and summed in bfloat16 or wider, within the bound.
No kernel may reach another device: no remote copies, remote signals or barrier semaphores. Data moves between devices by JAX's collectives and lax.ppermute only.
A program may use at most 192 MiB of HBM per device.

v0:
```python
import functools

import jax
import jax.numpy as jnp
import numpy as np
from jax import lax
from jax.experimental import pallas as pl
from jax.experimental.pallas import tpu as pltpu
from jax.sharding import PartitionSpec as P

KDIM = 128
VDIM = 256
SPAN = 64
LEVELS = 6
KINDS = LEVELS + 2
STEP_SPANS = 4
LANES = 128
LOWRANK = 16
DOWN_ROWS = slice(0, LOWRANK)
UP_ROWS = slice(LOWRANK, 2 * LOWRANK)
BIAS_ROWS = slice(2 * LOWRANK, 2 * LOWRANK + 8)
FEED_GAIN_ROW = 2 * LOWRANK + 8
MIXER_GAIN_ROW = FEED_GAIN_ROW + 1
PACKED_ROWS = FEED_GAIN_ROW + 8
UNPACK_FLOPS = 3 * 10**10

epsilon = 1e-06
head_epsilon = 1.0
gate_scale = 16.0
highest = lax.Precision.HIGHEST
f32 = jnp.float32
bf16 = jnp.bfloat16


def rms_forward(values, norm_gain, floor_value=epsilon):
    inverse = lax.rsqrt(jnp.mean(values * values, axis=-1, keepdims=True) + floor_value)
    return (values * inverse * norm_gain, inverse)


def rms_backward(values, inverse, norm_gain, upstream):
    scaled = upstream * norm_gain
    inner = jnp.mean(scaled * values, axis=-1, keepdims=True)
    grad_values = inverse * scaled - values * (inverse * inverse * inverse) * inner
    grad_gain = jnp.sum(upstream * values * inverse, axis=0)
    return (grad_values, grad_gain)


def group_layout(sequence_lengths, sequence_group, sequence_offset, which_group, places, span_count):
    live_record = (sequence_group == which_group) & (sequence_lengths > 0)
    start_row = sequence_offset * SPAN
    covered = (
        live_record[None, :]
        & (places >= start_row[None, :])
        & (places < (start_row + sequence_lengths)[None, :])
    )
    live_mask = jnp.any(covered, axis=1).astype(f32)
    span_ids = jnp.arange(span_count, dtype=jnp.int32)[:, None]
    restart = jnp.any(live_record[None, :] & (span_ids == sequence_offset[None, :]), axis=1)
    return (live_mask, restart.astype(jnp.int32))


def nn(left, right):
    return lax.dot_general(left, right, (((1,), (0,)), ((), ())), preferred_element_type=f32)


def nt(left, right):
    return lax.dot_general(left, right, (((1,), (1,)), ((), ())), preferred_element_type=f32)


def tn(left, right):
    return lax.dot_general(left, right, (((0,), (0,)), ((), ())), preferred_element_type=f32)


def decay_sums():
    rows = np.arange(SPAN)[:, None]
    cols = np.arange(SPAN)[None, :]
    blocks = [cols <= rows]
    for level in range(LEVELS):
        half = 1 << level
        edge = (rows // (2 * half)) * (2 * half) + half
        right = rows >= edge
        blocks.append(np.where(right, (cols >= edge) & (cols <= rows), (cols > rows) & (cols < edge)))
    blocks.append(cols > rows)
    return np.concatenate(blocks, axis=0).astype(np.float32)


def pair_levels():
    rows = lax.broadcasted_iota(jnp.int32, (SPAN, SPAN), 0)
    cols = lax.broadcasted_iota(jnp.int32, (SPAN, SPAN), 1)
    apart = rows ^ cols
    later = rows > cols
    masks = [later & (lax.shift_right_logical(apart, level) == 1) for level in range(LEVELS)]
    return masks, rows == cols


def span_factors(z_part, sums):
    decays = (jnp.minimum(z_part, 0.0) - jnp.log1p(jnp.exp(-jnp.abs(z_part)))) * (1.0 / gate_scale)
    high = decays.astype(bf16)
    low = (decays - high.astype(f32)).astype(bf16)
    return jnp.exp(nn(sums, jnp.concatenate([high, low], axis=0)))


def span_scores(queries, keys, factors, masks, diagonal):
    scores = jnp.where(diagonal, nt(queries.astype(bf16), keys.astype(bf16)), 0.0)
    query_levels = []
    key_levels = []
    for level in range(LEVELS):
        factor = factors[(level + 1) * SPAN : (level + 2) * SPAN]
        query_level = (queries * factor).astype(bf16)
        key_level = (keys * factor).astype(bf16)
        scores = jnp.where(masks[level], nt(query_level, key_level), scores)
        query_levels.append(query_level)
        key_levels.append(key_level)
    return scores, query_levels, key_levels


def forward_kernel(heads, scal, projected, z, live, gain, sums, gated, mixture, states, state):
    step = pl.program_id(0)
    key_width = heads * KDIM
    value_width = heads * VDIM

    @pl.when(step == 0)
    def _():
        state[...] = jnp.zeros_like(state)

    masks, diagonal = pair_levels()
    head_gain = gain[...]
    for part in range(STEP_SPANS):
        rows = slice(part * SPAN, (part + 1) * SPAN)
        factors_all = span_factors(z[rows, :], sums[...])
        keep = jnp.where(scal[1 + step * STEP_SPANS + part] == 0, 1.0, 0.0)
        for head in range(heads):
            keys_at = slice(head * KDIM, (head + 1) * KDIM)
            queries = projected[rows, keys_at].astype(f32)
            keys = projected[rows, key_width + head * KDIM : key_width + (head + 1) * KDIM].astype(f32)
            value_at = 2 * key_width + head * VDIM
            values = projected[rows, value_at : value_at + VDIM]
            gating = projected[rows, value_at + value_width : value_at + value_width + VDIM].astype(f32)
            factors = factors_all[:, keys_at]
            scores, _, _ = span_scores(queries, keys, factors, masks, diagonal)
            entering = state[head] * keep
            entering_low = entering.astype(bf16)
            states[part, head] = entering_low
            whole = factors[:SPAN]
            after = factors[(KINDS - 1) * SPAN :]
            mixed = nn(scores.astype(bf16), values) + nt(
                (queries * whole).astype(bf16), entering_low
            )
            state[head] = entering * whole[SPAN - 1 :] + tn(values, (keys * after).astype(bf16))
            value_cols = slice(head * VDIM, (head + 1) * VDIM)
            mixture[rows, value_cols] = mixed.astype(bf16)
            inverse = lax.rsqrt(jnp.mean(mixed * mixed, axis=-1, keepdims=True) + head_epsilon)
            silu = gating * jax.nn.sigmoid(gating)
            gated[rows, value_cols] = (mixed * inverse * head_gain * silu * live[rows, :]).astype(bf16)


def backward_kernel(
    heads,
    scal,
    projected,
    z,
    live,
    gain,
    sums,
    mixture,
    states,
    grad_gated,
    latent,
    up,
    normed,
    feed_gain_grad,
    grad_projected,
    packed,
    grad_up,
    grad_bias,
    grad_state,
):
    step = pl.program_id(0)
    natural = pl.num_programs(0) - 1 - step
    key_width = heads * KDIM
    value_width = heads * VDIM

    @pl.when(step == 0)
    def _():
        grad_state[...] = jnp.zeros_like(grad_state)
        packed[...] = jnp.zeros_like(packed)
        packed[FEED_GAIN_ROW : FEED_GAIN_ROW + 1, :] = feed_gain_grad[...]
        grad_up[...] = jnp.zeros_like(grad_up)
        grad_bias[...] = jnp.zeros_like(grad_bias)

    gain_at = slice(2 * key_width, 2 * key_width + VDIM)
    masks, diagonal = pair_levels()
    head_gain = gain[...]
    last_row = lax.broadcasted_iota(jnp.int32, (SPAN, KDIM), 0) == SPAN - 1
    for part in reversed(range(STEP_SPANS)):
        rows = slice(part * SPAN, (part + 1) * SPAN)
        z_part = z[rows, :]
        factors_all = span_factors(z_part, sums[...])
        keep = jnp.where(scal[1 + natural * STEP_SPANS + part] == 0, 1.0, 0.0)
        live_part = live[rows, :]
        exponents = []
        for head in range(heads):
            keys_at = slice(head * KDIM, (head + 1) * KDIM)
            key_cols = slice(key_width + head * KDIM, key_width + (head + 1) * KDIM)
            value_at = 2 * key_width + head * VDIM
            value_cols = slice(value_at, value_at + VDIM)
            gate_cols = slice(value_at + value_width, value_at + value_width + VDIM)
            mixed_cols = slice(head * VDIM, (head + 1) * VDIM)
            queries = projected[rows, keys_at].astype(f32)
            keys = projected[rows, key_cols].astype(f32)
            values = projected[rows, value_cols]
            gating = projected[rows, gate_cols].astype(f32)
            factors = factors_all[:, keys_at]
            scores, query_levels, key_levels = span_scores(queries, keys, factors, masks, diagonal)
            scores_low = scores.astype(bf16)
            whole = factors[:SPAN]
            after = factors[(KINDS - 1) * SPAN :]

            mixed = mixture[rows, mixed_cols].astype(f32)
            inverse = lax.rsqrt(jnp.mean(mixed * mixed, axis=-1, keepdims=True) + head_epsilon)
            unit = mixed * inverse
            sigmoid = jax.nn.sigmoid(gating)
            silu = gating * sigmoid
            upstream = grad_gated[rows, mixed_cols].astype(f32) * live_part
            grad_projected[rows, gate_cols] = (
                upstream * unit * head_gain * (sigmoid + silu * (1.0 - sigmoid))
            ).astype(bf16)
            normed_back = upstream * silu
            gain_part = normed_back * unit
            packed[BIAS_ROWS, gain_at] += jnp.sum(gain_part.reshape(SPAN // 8, 8, VDIM), axis=0)
            scaled = normed_back * head_gain
            inner = jnp.mean(scaled * unit, axis=-1, keepdims=True)
            grad_mixed = (inverse * (scaled - unit * inner)).astype(bf16)

            entering = states[part, head]
            leaving = grad_state[head]
            leaving_low = leaving.astype(bf16)
            grad_scores = nt(grad_mixed, values)
            after_keys = (keys * after).astype(bf16)
            whole_queries = (queries * whole).astype(bf16)
            grad_projected[rows, value_cols] = (
                tn(scores_low, grad_mixed) + nt(after_keys, leaving_low)
            ).astype(bf16)
            grad_queries = whole * nn(grad_mixed, entering)
            grad_keys = after * nn(values, leaving_low)
            fading = whole[SPAN - 1 :]
            last_sum = fading * jnp.sum(entering.astype(f32) * leaving, axis=0, keepdims=True)
            exponents_head = [queries * grad_queries + jnp.where(last_row, last_sum, 0.0)]
            last_exponent = keys * grad_keys
            for level in range(LEVELS):
                factor = factors[(level + 1) * SPAN : (level + 2) * SPAN]
                level_back = jnp.where(masks[level], grad_scores, 0.0).astype(bf16)
                query_part = factor * nn(level_back, key_levels[level])
                key_part = factor * tn(level_back, query_levels[level])
                grad_queries += query_part
                grad_keys += key_part
                exponents_head.append(queries * query_part + keys * key_part)
            exponents_head.append(last_exponent)
            same = jnp.sum(jnp.where(diagonal, grad_scores, 0.0), axis=1, keepdims=True)
            grad_projected[rows, keys_at] = (grad_queries + same * keys).astype(bf16)
            grad_projected[rows, key_cols] = (grad_keys + same * queries).astype(bf16)
            exponents.append(jnp.concatenate(exponents_head, axis=0).astype(bf16))
            grad_state[head] = keep * (leaving * fading + tn(grad_mixed, whole_queries))
        grad_decays = tn(sums[:, :SPAN], jnp.concatenate(exponents, axis=1))
        grad_z = grad_decays * jax.nn.sigmoid(-z_part) * (1.0 / gate_scale)
        grad_bias[...] += jnp.sum(grad_z.reshape(SPAN // 8, 8, key_width), axis=0)
        grad_z_low = grad_z.astype(bf16)
        grad_up[...] += tn(latent[rows, :LOWRANK], grad_z_low)
        latent_cols = slice(2 * key_width + 2 * value_width, grad_projected.shape[1])
        grad_projected[rows, latent_cols] = nt(grad_z_low, up[...]).astype(bf16)

    latent_at = 2 * key_width + 2 * value_width
    packed[DOWN_ROWS, :] += tn(grad_projected[:, latent_at : latent_at + LOWRANK], normed[...])

    for half in range(2):

        @pl.when((step == pl.num_programs(0) - 1) & (scal[0] == half))
        def _(at=slice(half * key_width, (half + 1) * key_width)):
            packed[UP_ROWS, at] = grad_up[...]
            packed[BIAS_ROWS, at] = grad_bias[...]


def mixer_specs(length, projected_width, key_width, value_width, width, reverse):
    steps = length // (SPAN * STEP_SPANS)
    step_rows = SPAN * STEP_SPANS
    heads = key_width // KDIM

    def natural(step):
        return steps - 1 - step if reverse else step

    def by_rows(step, scal):
        return (lax.rem(natural(step) + scal[0] * (steps // 2), steps), 0)

    def whole(step, scal):
        return (0, 0)

    return dict(
        steps=steps,
        projected=pl.BlockSpec((step_rows, projected_width), by_rows),
        z=pl.BlockSpec((step_rows, key_width), by_rows),
        live=pl.BlockSpec((step_rows, 1), by_rows),
        gain=pl.BlockSpec((1, VDIM), whole),
        sums=pl.BlockSpec((KINDS * SPAN, 2 * SPAN), whole),
        values=pl.BlockSpec((step_rows, value_width), by_rows),
        states=pl.BlockSpec(
            (STEP_SPANS, heads, VDIM, KDIM), lambda step, scal: (natural(step), 0, 0, 0)
        ),
        normed=pl.BlockSpec((step_rows, width), by_rows),
        feed_gain=pl.BlockSpec((1, width), whole),
        packed=pl.BlockSpec((PACKED_ROWS, width), whole),
        latent=pl.BlockSpec((step_rows, LANES), by_rows),
        up=pl.BlockSpec((LANES, key_width), whole),
        extended=pl.BlockSpec((step_rows, projected_width + LANES), by_rows),
    )


def mixer_forward(scal, projected, z, live, gain, sums):
    length, projected_width = projected.shape
    key_width = z.shape[1]
    heads = key_width // KDIM
    value_width = heads * VDIM
    spans = length // SPAN
    specs = mixer_specs(length, projected_width, key_width, value_width, LANES, False)
    return pl.pallas_call(
        functools.partial(forward_kernel, heads),
        grid_spec=pltpu.PrefetchScalarGridSpec(
            num_scalar_prefetch=1,
            grid=(specs["steps"],),
            in_specs=[specs[name] for name in ("projected", "z", "live", "gain", "sums")],
            out_specs=[specs[name] for name in ("values", "values", "states")],
            scratch_shapes=[pltpu.VMEM((heads, VDIM, KDIM), f32)],
        ),
        out_shape=[
            jax.ShapeDtypeStruct((length, value_width), bf16),
            jax.ShapeDtypeStruct((length, value_width), bf16),
            jax.ShapeDtypeStruct((spans, heads, VDIM, KDIM), bf16),
        ],
        compiler_params=pltpu.CompilerParams(vmem_limit_bytes=40 * 1024 * 1024),
        cost_estimate=pl.CostEstimate(
            flops=10**10, bytes_accessed=15 * 10**6, transcendentals=4 * 10**6
        ),
        name="mixer_forward",
    )(scal, projected, z, live, gain, sums)


def mixer_backward(
    scal,
    projected,
    z,
    live,
    gain,
    sums,
    mixture,
    states,
    grad_gated,
    latent,
    up,
    normed,
    feed_gain_grad,
):
    length, projected_width = projected.shape
    key_width = z.shape[1]
    heads = key_width // KDIM
    value_width = heads * VDIM
    width = normed.shape[1]
    specs = mixer_specs(length, projected_width, key_width, value_width, width, True)
    names = ("projected", "z", "live", "gain", "sums", "values", "states", "values")
    names += ("latent", "up", "normed", "feed_gain")
    return pl.pallas_call(
        functools.partial(backward_kernel, heads),
        grid_spec=pltpu.PrefetchScalarGridSpec(
            num_scalar_prefetch=1,
            grid=(specs["steps"],),
            in_specs=[specs[name] for name in names],
            out_specs=[specs[name] for name in ("extended", "packed")],
            scratch_shapes=[
                pltpu.VMEM((LOWRANK, key_width), f32),
                pltpu.VMEM((8, key_width), f32),
                pltpu.VMEM((heads, VDIM, KDIM), f32),
            ],
        ),
        out_shape=[
            jax.ShapeDtypeStruct((length, projected_width + LANES), bf16),
            jax.ShapeDtypeStruct((PACKED_ROWS, width), f32),
        ],
        compiler_params=pltpu.CompilerParams(vmem_limit_bytes=40 * 1024 * 1024),
        cost_estimate=pl.CostEstimate(
            flops=25 * 10**9, bytes_accessed=20 * 10**6, transcendentals=4 * 10**6
        ),
        name="mixer_backward",
    )(
        scal,
        projected,
        z,
        live,
        gain,
        sums,
        mixture,
        states,
        grad_gated,
        latent,
        up,
        normed,
        feed_gain_grad,
    )


def unpack_kernel(packed, *parts):
    width = parts[0].shape[1]
    for index, part in enumerate(parts):
        part[...] = packed[:, index * width : (index + 1) * width].astype(f32)


def unpack_thirds(packed):
    rows, width = packed.shape[0], packed.shape[1] // 3
    return pl.pallas_call(
        unpack_kernel,
        out_shape=[jax.ShapeDtypeStruct((rows, width), f32)] * 3,
        compiler_params=pltpu.CompilerParams(vmem_limit_bytes=8 * 1024 * 1024),
        cost_estimate=pl.CostEstimate(
            flops=UNPACK_FLOPS, bytes_accessed=3 * 10**6, transcendentals=0
        ),
        name="unpack_thirds",
    )(packed)


def lane_pad(values, axis):
    widths = [(0, 0), (0, 0)]
    widths[axis] = (0, LANES - values.shape[axis])
    return jnp.pad(values, widths)


def swap_tensor(values):
    return lax.ppermute(values, "tensor", [(0, 1), (1, 0)])


def chip_sum(values):
    count = lax.axis_size("dp")
    parity = lax.axis_index("dp") % 2
    blocks = values.reshape(count // 2, 2, values.shape[0] // count, values.shape[1])
    kept = lax.dynamic_index_in_dim(blocks, parity, 1, keepdims=False)
    sent = lax.dynamic_index_in_dim(blocks, 1 - parity, 1, keepdims=False)
    arrived = lax.ppermute(sent, "dp", [(i, i ^ 1) for i in range(count)])
    total = (kept.astype(f32) + arrived.astype(f32)).astype(bf16)
    return total.reshape(values.shape[0] // 2, values.shape[1])


def halving_stages():
    return (lax.axis_size("dp") // 2).bit_length() - 1


def by_chip(values):
    stages = halving_stages()
    return values.reshape((2,) * stages + (values.shape[0] >> stages, values.shape[1]))


def halving_stage(held, stage):
    count = lax.axis_size("dp")
    stages = halving_stages()
    bit = 2 << stage
    side = (lax.axis_index("dp") // bit) % 2
    axis = stages - 1 - stage
    kept = lax.dynamic_index_in_dim(held, side, axis, keepdims=False)
    sent = lax.dynamic_index_in_dim(held, 1 - side, axis, keepdims=False)
    arrived = lax.ppermute(sent, "dp", [(i, i ^ bit) for i in range(count)])
    total = kept.astype(f32) + arrived.astype(f32)
    return total if stage == stages - 1 else total.astype(bf16)


def halving_rest(held, first):
    for stage in range(first, halving_stages()):
        held = halving_stage(held, stage)
    return held


def both_ways(side, mine, other, axis):
    first = jnp.where(side == 0, mine, other)
    second = jnp.where(side == 0, other, mine)
    return jnp.stack([first, second], axis=axis)


def swap_half(values):
    half = values.shape[0] // 2
    parity = lax.axis_index("dp") % 2
    return swap_tensor(lax.dynamic_slice_in_dim(values, parity * half, half, 0))


def join_halves(mine):
    count = lax.axis_size("dp")
    parity = lax.axis_index("dp") % 2
    other = lax.ppermute(mine, "dp", [(i, i ^ 1) for i in range(count)])
    return both_ways(parity, mine, other, 0).reshape(mine.shape[0] * 2, mine.shape[1])


def butterfly_sum(values):
    count = lax.axis_size("dp")
    reaches = [1 << bit for bit in range(count.bit_length() - 1)]
    total = values
    for reach in reaches[:1] + reaches[2:] + reaches[1:2]:
        low = total.astype(bf16)
        arrived = lax.ppermute(low, "dp", [(i, i ^ reach) for i in range(count)])
        total = low.astype(f32) + arrived.astype(f32)
    low = total.astype(bf16)
    return low.astype(f32) + swap_tensor(low).astype(f32)


def on_device(
    tokens,
    cotangent,
    sequence_lengths,
    sequence_group,
    sequence_offset,
    mixer_gain,
    query_weight,
    key_weight,
    value_weight,
    output_gate,
    output_weight,
    decay_down,
    decay_up,
    decay_bias,
    head_gain,
    feed_gain,
    feed_gate,
    feed_up,
    feed_down,
):
    which_group = lax.axis_index("dp")
    half_index = lax.axis_index("tensor")
    own = tokens.shape[0]
    group_rows = own * 2
    key_width = query_weight.shape[1]
    value_width = value_weight.shape[1]
    feed_width = feed_gate.shape[1]
    places = (jnp.arange(group_rows, dtype=jnp.int32) + half_index * own) % group_rows
    live_mask, restart = group_layout(
        sequence_lengths,
        sequence_group,
        sequence_offset,
        which_group,
        places[:, None],
        group_rows // SPAN,
    )
    live = live_mask[:, None]
    scal = jnp.concatenate([half_index.astype(jnp.int32)[None], restart])
    sums = jnp.asarray(np.tile(decay_sums(), (1, 2)), bf16)
    gain_head = head_gain.astype(f32)[None, :]

    joined = lax.all_gather(
        jnp.concatenate(
            [query_weight, key_weight, value_weight, output_gate, output_weight], axis=1
        ),
        "dp",
        axis=0,
        tiled=True,
    )
    feed_all = lax.all_gather(
        jnp.concatenate([feed_gate, feed_up, feed_down], axis=1), "dp", axis=0, tiled=True
    )
    gate_up_full = feed_all[:, : 2 * feed_width]
    feed_down_full = feed_all[:, 2 * feed_width :]
    gain_in = mixer_gain.astype(f32)
    token_values = tokens.astype(f32)
    normed_in, inverse_in = rms_forward(token_values, gain_in)
    normed_low = normed_in.astype(bf16)
    normed_other = swap_tensor(normed_low)
    cotangent_other = swap_tensor(cotangent)
    joined, cotangent_other = lax.optimization_barrier((joined, cotangent_other))
    projected_width = 2 * key_width + 2 * value_width
    joined_in = joined[:, :projected_width]
    output_half = joined[:, projected_width:]
    output_piece = swap_half(output_half)

    normed_all = jnp.concatenate([normed_low, normed_other], axis=0)
    projected = nn(normed_all, joined_in).astype(bf16)
    latent = nn(normed_all, decay_down)
    up_local = lax.dynamic_slice_in_dim(decay_up, half_index * key_width, key_width, 1).astype(f32)
    bias_local = lax.dynamic_slice_in_dim(decay_bias, half_index * key_width, key_width, 0)
    z = jnp.dot(latent, up_local, precision=highest) + bias_local.astype(f32)
    gated, mixture, states = mixer_forward(scal, projected, z, live, gain_head, sums)

    gated, output_piece = lax.optimization_barrier((gated, output_piece))
    output_other = join_halves(output_piece)
    gated_own = gated[:own]
    gated_rest = swap_tensor(gated[own:])
    attended = nt(gated_own, output_half) + nt(gated_rest, output_other)
    middle = token_values + attended
    gain_mid = feed_gain.astype(f32)
    normed_mid, inverse_mid = rms_forward(middle, gain_mid)
    mid_low = normed_mid.astype(bf16)
    mid_other = swap_tensor(mid_low)

    def feed_rows(mid_rows, cotangent_rows):
        both = nn(mid_rows, gate_up_full)
        gate_part = both[:, :feed_width]
        up_part = both[:, feed_width:]
        sigmoid_gate = jax.nn.sigmoid(gate_part)
        silu_gate = gate_part * sigmoid_gate
        hidden_low = (silu_gate * up_part).astype(bf16)
        grad_hidden = nn(cotangent_rows, feed_down_full)
        grad_gate_low = (
            grad_hidden * up_part * (sigmoid_gate + silu_gate * (1.0 - sigmoid_gate))
        ).astype(bf16)
        grad_up_low = (grad_hidden * silu_gate).astype(bf16)
        grad_both = jnp.concatenate([grad_gate_low, grad_up_low], axis=1)
        return hidden_low, grad_both, nt(grad_both, gate_up_full)

    hidden_other, grad_both_other, mid_back_other = feed_rows(mid_other, cotangent_other)
    mid_send, mid_here, cotangent_here = lax.optimization_barrier(
        (mid_back_other.astype(bf16), mid_low, cotangent)
    )
    mid_back = swap_tensor(mid_send)
    hidden_own, grad_both_own, mid_back_own = feed_rows(mid_here, cotangent_here)

    upstream = cotangent.astype(f32)
    grad_normed_mid = mid_back_own + mid_back.astype(f32)
    grad_mid_in, grad_feed_gain = rms_backward(middle, inverse_mid, gain_mid, grad_normed_mid)
    grad_middle = upstream + grad_mid_in
    grad_attended = grad_middle.astype(bf16)
    gated_send, attended_late, hidden_late = lax.optimization_barrier(
        (nn(grad_attended, output_other).astype(bf16), grad_attended, hidden_other)
    )
    gated_back = swap_tensor(gated_send)
    grad_gated = jnp.concatenate([nn(attended_late, output_half).astype(bf16), gated_back], axis=0)
    fed_send = nt(hidden_late, feed_down_full).astype(bf16)
    output_grads = tn(attended_late, jnp.concatenate([gated_own, gated_rest], axis=1)).astype(bf16)
    grad_gated, fed_send, output_grads = lax.optimization_barrier(
        (grad_gated, fed_send, output_grads)
    )
    fed_back = swap_tensor(fed_send)

    mid_all = jnp.concatenate([mid_low, mid_other], axis=0)
    cotangent_all = jnp.concatenate([cotangent, cotangent_other], axis=0)
    hidden_all = jnp.concatenate([hidden_own, hidden_other], axis=0)
    grad_both_all = jnp.concatenate([grad_both_own, grad_both_other], axis=0)
    feed_grads = jnp.concatenate(
        [
            tn(mid_all, grad_both_all).astype(bf16),
            tn(cotangent_all, hidden_all).astype(bf16),
        ],
        axis=1,
    )
    feed_sum = lax.psum_scatter(feed_grads, "dp", scatter_dimension=0, tiled=True)
    grad_projected, packed = mixer_backward(
        scal,
        projected,
        z,
        live,
        gain_head,
        sums,
        mixture,
        states,
        grad_gated,
        lane_pad(latent, 1).astype(bf16),
        lane_pad(up_local, 0).astype(bf16),
        normed_all,
        grad_feed_gain[None, :],
    )
    grad_joined = tn(normed_all, grad_projected).astype(bf16)
    grad_joined, output_grads, fed_back = lax.optimization_barrier(
        (grad_joined, output_grads, fed_back)
    )
    projected_chip, hidden_last = lax.optimization_barrier(
        (chip_sum(grad_joined[:, :projected_width]), hidden_own)
    )
    joined_sums = [
        halving_stage(by_chip(piece), 0) for piece in jnp.split(projected_chip, 2, axis=1)
    ]
    output_chip = chip_sum(output_grads)
    output_back = swap_tensor(output_chip[:, value_width:])
    joined_back = jnp.concatenate([joined_in, lane_pad(decay_down, 1)], axis=1)
    normed_part = nt(grad_projected, joined_back)
    grad_mixer_gain = jnp.sum(normed_part * normed_all.astype(f32), axis=0) / gain_in
    normed_part, _ = lax.optimization_barrier((normed_part.astype(bf16), output_back))
    fed = nt(hidden_last, feed_down_full) + fed_back.astype(f32)
    output = (middle + fed).astype(bf16)
    output_total = output_chip[:, :value_width].astype(f32) + output_back.astype(f32)
    joined_sums.append(halving_stage(by_chip(output_total.astype(bf16)), 0))
    packed, _ = lax.optimization_barrier((packed, joined_sums[0]))
    joined_sums = [halving_stage(held, 1) for held in joined_sums]
    normed_back, _ = lax.optimization_barrier((swap_tensor(normed_part[own:]), joined_sums[1]))
    grad_normed = normed_part[:own].astype(f32) + normed_back.astype(f32)
    grad_in_part = rms_backward(token_values, inverse_in, gain_in, grad_normed)[0]
    input_grad = grad_middle + grad_in_part

    flat = lax.dynamic_update_slice_in_dim(packed, grad_mixer_gain[None, :], MIXER_GAIN_ROW, 0)
    flat = butterfly_sum(flat)
    joined_sum = jnp.concatenate([halving_rest(held, 2) for held in joined_sums], axis=1)
    channels = 2 * key_width
    return (
        output,
        input_grad,
        flat[MIXER_GAIN_ROW],
        joined_sum[:, :key_width],
        joined_sum[:, key_width : 2 * key_width],
        joined_sum[:, 2 * key_width : 2 * key_width + value_width],
        joined_sum[:, 2 * key_width + value_width : projected_width],
        joined_sum[:, projected_width:],
        flat[DOWN_ROWS].T,
        flat[UP_ROWS, :channels],
        jnp.sum(flat[BIAS_ROWS, :channels], axis=0),
        jnp.sum(flat[BIAS_ROWS, channels : channels + VDIM], axis=0),
        flat[FEED_GAIN_ROW],
        *unpack_thirds(feed_sum),
    )


def solution(mesh):
    rows = P(("dp", "tensor"), None)
    weight = P("dp", "tensor")
    return jax.shard_map(
        on_device,
        mesh=mesh,
        in_specs=(rows, rows, P(), P(), P(), P())
        + (weight,) * 5
        + (P(), P(), P(), P(), P())
        + (weight,) * 3,
        out_specs=(rows, rows, P()) + (weight,) * 5 + (P(),) * 5 + (weight,) * 3,
        check_vma=False,
    )
```

profile of v0, /device:TPU:0, one launch (start us, length us, event | category | flops | bytes accessed | tf_op | source)
XLA Modules:
  0.0 358.6 jit_solution(8581658232290090797)
XLA Ops:
  20.8 22.4 %collective-permute-done = bf16[512,1024]{1,0:T(8,128)(2,1)} collective-permute-done((bf16[512,1024]{1,0:T(8,128)(2,1)S(1)}, bf16[512,1024]{1,0:T(8,128)(2,1)}, u32[]{:S(2)}, u32[]{:S(2)}) %collective-permute-start) | collective-permute-done | bytes 1048608 | tf_op jit(solution)/shard_map/ppermute | solution.py:434
  46.9 18.0 %collective-permute-done.1 = bf16[512,1024]{1,0:T(8,128)(2,1)} collective-permute-done((bf16[512,1024]{1,0:T(8,128)(2,1)}, bf16[512,1024]{1,0:T(8,128)(2,1)}, u32[]{:S(2)}, u32[]{:S(2)}) %collective-permute-start.1) | collective-permute-done | bytes 1048608 | tf_op jit(solution)/shard_map/ppermute | solution.py:434
  68.5 5.5 %convolution_convert_fusion.2.projected = bf16[1024,1536]{1,0:T(8,128)(2,1)S(1)} fusion(bf16[1024,1024]{1,0:T(8,128)(2,1)S(1)} %pad_maximum_fusion.1.normed, bf16[1024,2048]{1,0:T(8,128)(2,1)} %all-gather.3.cloned.1.call-done), kind=kOutput, calls=%fused_computation.20 | convolution fusion | flops 3222798336 | bytes 8388608 | tf_op jit(solution)/shard_map/dot_general | solution.py:63
  74.1 9.4 %mixer_forward.1 = (bf16[1024,512]{1,0:T(8,128)(2,1)S(1)}, bf16[1024,512]{1,0:T(8,128)(2,1)S(1)}, bf16[16,2,256,128]{3,2,1,0:T(8,128)(2,1)S(1)}) custom-call(s32[17]{0:T(128)S(1)} %pad_add_fusion.scal, bf16[1024,1536]{1,0:T(8,128)(2,1)S(1)} %convolution_convert_fusion.2.projected, f32[1024,256]{1,0:T(8,128)S(1)} %copy-done.2, f32[1024,1]{1,0:T(8,128)S(1)} %copy-done.4, ...), custom_call_target="tpu_custom_call" | custom-call | flops 10000000000 | bytes 15000000 | tf_op jit(solution)/shard_map/mixer_forward/pallas_call | solution.py:324
  89.5 12.0 %collective-permute-done.3 = bf16[512,512]{1,0:T(8,128)(2,1)} collective-permute-done((bf16[512,512]{1,0:T(8,128)(2,1)}, bf16[512,512]{1,0:T(8,128)(2,1)}, u32[]{:S(2)}, u32[]{:S(2)}) %collective-permute-start.3) | collective-permute-done | bytes 524320 | tf_op jit(solution)/shard_map/ppermute | solution.py:434
  108.1 23.8 %collective-permute-done.5 = bf16[512,1024]{1,0:T(8,128)(2,1)} collective-permute-done((bf16[512,1024]{1,0:T(8,128)(2,1)}, bf16[512,1024]{1,0:T(8,128)(2,1)}, u32[]{:S(2)}, u32[]{:S(2)}) %collective-permute-start.5) | collective-permute-done | bytes 1048608 | tf_op jit(solution)/shard_map/ppermute | solution.py:434
  132.0 11.0 %all-gather.5.cloned.1.call-done = bf16[1024,4224]{1,0:T(8,128)(2,1)} async-done(((bf16[64,4224]{1,0:T(8,128)(2,1)}), bf16[1024,4224]{1,0:T(8,128)(2,1)}) %all-gather.5.cloned.1.call-update) | async-done | bytes 8650768 | tf_op jit(solution)/shard_map/all_gather | solution.py:557
  142.9 6.2 %fusion.18 = f32[512,2816]{1,0:T(8,128)S(1)} fusion(bf16[512,1024]{1,0:T(8,128)(2,1)} %collective-permute-done.5, bf16[1024,4224]{1,0:T(8,128)(2,1)} %all-gather.5.cloned.1.call-done), kind=kOutput, calls=%fused_computation.27 | convolution fusion | flops 2952790016 | bytes 12582912 | tf_op jit(solution)/shard_map/dot_general | solution.py:63
  149.2 15.4 %multiply_convert_fusion.5 = (bf16[512,1408]{1,0:T(8,128)(2,1)S(1)}, bf16[512,1408]{1,0:T(8,128)(2,1)S(1)}, bf16[512,1408]{1,0:T(8,128)(2,1)}) fusion(f32[512,2816]{1,0:T(8,128)S(1)} %fusion.18, bf16[512,1024]{1,0:T(8,128)(2,1)} %collective-permute-done.1, bf16[1024,4224]{1,0:T(8,128)(2,1)S(1)} %copy-done.40), kind=kOutput, calls=%fused_computation.51 | convolution fusion | flops 1486487552 | bytes 14024704 | tf_op jit(solution)/shard_map/dot_general | solution.py:63
  164.6 4.2 %fusion.62 = bf16[512,1024]{1,0:T(8,128)(2,1)} fusion(bf16[1024,4224]{1,0:T(8,128)(2,1)S(1)} %copy-done.40, bf16[512,1408]{1,0:T(8,128)(2,1)S(1)} %get-tuple-element.81, bf16[512,1408]{1,0:T(8,128)(2,1)S(1)} %get-tuple-element.80), kind=kOutput, calls=%fused_computation.91 | convolution fusion | flops 2959081472 | bytes 9699328 | tf_op jit(solution)/shard_map/dot_general | solution.py:67
  170.3 4.4 %fusion.14 = f32[512,2816]{1,0:T(8,128)S(1)} fusion(bf16[512,1024]{1,0:T(8,128)(2,1)} %multiply_convert_fusion.6, bf16[1024,4224]{1,0:T(8,128)(2,1)S(1)} %copy-done.40), kind=kOutput, calls=%fused_computation.23 | convolution fusion | flops 2952790016 | bytes 12582912 | tf_op jit(solution)/shard_map/dot_general | solution.py:63
  174.7 4.1 %multiply_convert_fusion.3 = (bf16[512,1408]{1,0:T(8,128)(2,1)S(1)}, bf16[512,1408]{1,0:T(8,128)(2,1)S(1)}, bf16[512,1408]{1,0:T(8,128)(2,1)S(1)}) fusion(f32[512,2816]{1,0:T(8,128)S(1)} %fusion.14, bf16[512,1024]{1,0:T(8,128)(2,1)} %param.21, bf16[1024,4224]{1,0:T(8,128)(2,1)S(1)} %copy-done.40), kind=kOutput, calls=%fused_computation.48 | convolution fusion | flops 1486487552 | bytes 14024704 | tf_op jit(solution)/shard_map/dot_general | solution.py:63
  178.8 10.2 %fusion.9 = bf16[1024,2816]{1,0:T(8,128)(2,1)S(1)} fusion(bf16[512,1408]{1,0:T(8,128)(2,1)} %copy-done.49, bf16[512,1408]{1,0:T(8,128)(2,1)} %copy-done.48, bf16[512,1408]{1,0:T(8,128)(2,1)S(1)} %get-tuple-element.79, bf16[512,1408]{1,0:T(8,128)(2,1)S(1)} %get-tuple-element.78, bf16[512,1024]{1,0:T(8,128)(2,1)} %collective-permute-done.5, ...), kind=kOutput, calls=%fused_computation.11 | convolution fusion | flops 5935726592 | bytes 13631488 | tf_op jit(solution)/shard_map/dot_general | solution.py:71
  189.1 5.5 %convolution_convert_fusion.1 = bf16[1024,1408]{1,0:T(8,128)(2,1)S(1)} fusion(bf16[512,1408]{1,0:T(8,128)(2,1)} %get-tuple-element.57, bf16[512,1408]{1,0:T(8,128)(2,1)S(1)} %get-tuple-element.63, bf16[512,1024]{1,0:T(8,128)(2,1)} %collective-permute-done.1, bf16[512,1024]{1,0:T(8,128)(2,1)} %param.21), kind=kOutput, calls=%fused_computation.19 | convolution fusion | flops 2964193280 | bytes 7864320 | tf_op jit(solution)/shard_map/dot_general | solution.py:71
  194.6 4.2 %pad_maximum_fusion = bf16[1024,4224]{1,0:T(8,128)(2,1)} fusion(bf16[1024,1408]{1,0:T(8,128)(2,1)S(1)} %convolution_convert_fusion.1, bf16[1024,2816]{1,0:T(8,128)(2,1)S(1)} %fusion.9), kind=kLoop, calls=%fused_computation | loop fusion | flops 17301504 | bytes 17301504 | tf_op jit(solution)/shard_map/concatenate | solution.py:636
  198.8 8.4 %multiply_reduce_fusion.1 = (f32[1024]{0:T(1024)S(1)}, f32[512]{0:T(512)S(1)}, f32[512,1024]{1,0:T(8,128)S(1)}) fusion(f32[512,1024]{1,0:T(8,128)} %copy-done.14, f32[512]{0:T(512)S(1)} %get-tuple-element.103, bf16[512,1024]{1,0:T(8,128)(2,1)} %collective-permute-done.6, f32[1024]{0:T(1024)S(1)} %convert_element_type.302, ...), kind=kOutput, calls=%fused_computation.73 | convolution fusion | flops 2962749952 | bytes 13905920 | tf_op jit(solution)/shard_map/dot_general | solution.py:67
  216.7 4.0 %fusion.59 = bf16[512,1024]{1,0:T(8,128)(2,1)S(1)} fusion(bf16[512,1408]{1,0:T(8,128)(2,1)S(1)} %copy-done.44, bf16[1024,4224]{1,0:T(8,128)(2,1)} %all-gather.5.cloned.1.call-done), kind=kOutput, calls=%fused_computation.90 | convolution fusion | flops 1476919296 | bytes 5373952 | tf_op jit(solution)/shard_map/dot_general | solution.py:67
  220.8 4.9 %collective-permute-done.7 = bf16[512,512]{1,0:T(8,128)(2,1)S(1)} collective-permute-done((bf16[512,512]{1,0:T(8,128)(2,1)S(1)}, bf16[512,512]{1,0:T(8,128)(2,1)S(1)}, u32[]{:S(2)}, u32[]{:S(2)}) %collective-permute-start.7) | collective-permute-done | bytes 524320 | tf_op jit(solution)/shard_map/ppermute | solution.py:434
  226.1 21.3 %mixer_backward.1 = (bf16[1024,1664]{1,0:T(8,128)(2,1)}, f32[48,1024]{1,0:T(8,128)S(1)}) custom-call(s32[17]{0:T(128)S(1)} %pad_add_fusion.scal, bf16[1024,1536]{1,0:T(8,128)(2,1)S(1)} %copy-done.9, f32[1024,256]{1,0:T(8,128)S(1)} %copy-done.3, f32[1024,1]{1,0:T(8,128)S(1)} %copy-done.5, f32[1,256]{1,0:T(1,128)S(1)} %bitcast.100, ...), custom_call_target="tpu_custom_call" | custom-call | flops 24999999488 | bytes 20000000 | tf_op jit(solution)/shard_map/mixer_backward/pallas_call | solution.py:369
  247.5 6.4 %convolution_convert_fusion = bf16[1024,1664]{1,0:T(8,128)(2,1)S(1)} fusion(bf16[1024,1024]{1,0:T(8,128)(2,1)S(1)} %pad_maximum_fusion.1.normed, bf16[1024,1664]{1,0:T(8,128)(2,1)} %get-tuple-element.59), kind=kOutput, calls=%fused_computation.18 | convolution fusion | flops 3491364864 | bytes 8912896 | tf_op jit(solution)/shard_map/dot_general | solution.py:71
  256.9 4.2 %multiply_reduce_fusion = (f32[1024]{0:T(1024)S(1)}, bf16[1024,1024]{1,0:T(8,128)(2,1)S(1)}) fusion(bf16[1024,1024]{1,0:T(8,128)(2,1)S(1)} %pad_maximum_fusion.1.normed, bf16[1024,1664]{1,0:T(8,128)(2,1)S(1)} %copy-done.45, bf16[1024,16]{1,0:T(8,128)(2,1)S(1)} %copy.57, bf16[1024,1536]{1,0:T(8,128)(2,1)S(1)} %slice-done), kind=kOutput, calls=%fused_computation.12 | convolution fusion | flops 3504077824 | bytes 10784768 | tf_op jit(solution)/shard_map/dot_general | solution.py:67
  264.0 10.5 %collective-permute-done.11 = bf16[512,512]{1,0:T(8,128)(2,1)S(1)} collective-permute-done((bf16[512,512]{1,0:T(8,128)(2,1)S(1)}, bf16[512,512]{1,0:T(8,128)(2,1)S(1)}, u32[]{:S(2)}, u32[]{:S(2)}) %collective-permute-start.11) | collective-permute-done | bytes 524320 | tf_op jit(solution)/shard_map/ppermute | solution.py:434
  284.3 20.8 %collective-permute-done.24 = bf16[2,2,64,512]{3,2,1,0:T(8,128)(2,1)S(1)} collective-permute-done((bf16[2,2,64,512]{3,2,1,0:T(8,128)(2,1)S(1)}, bf16[2,2,64,512]{3,2,1,0:T(8,128)(2,1)S(1)}, u32[]{:S(2)}, u32[]{:S(2)}) %collective-permute-start.24) | collective-permute-done | bytes 262176 | tf_op jit(solution)/shard_map/ppermute | solution.py:465
  314.6 4.1 %collective-permute-done.26 = bf16[64,512]{1,0:T(8,128)(2,1)S(1)} collective-permute-done((bf16[64,512]{1,0:T(8,128)(2,1)S(1)}, bf16[64,512]{1,0:T(8,128)(2,1)S(1)}, u32[]{:S(2)}, u32[]{:S(2)}) %collective-permute-start.26) | collective-permute-done | bytes 65568 | tf_op jit(solution)/shard_map/ppermute | solution.py:465
  (250 shorter events, 102.4 us)
Async XLA Ops:
  7.2 58.3 %all-gather.3.cloned.1.call-start = ((), (), s32[]{:S(2)}) async-start(), calls=%async_computation.1 | async-start | bytes 4456448 | tf_op jit(solution)/shard_map/all_gather | solution.py:549
  12.2 130.8 %all-gather.5.cloned.1.call-start = ((), (), s32[]{:S(2)}) async-start(), calls=%async_computation.2 | async-start | bytes 9191424 | tf_op jit(solution)/shard_map/all_gather | solution.py:557
  14.2 335.6 %reduce-scatter.2.cloned.1.call-start = ((), (), s32[]{:S(2)}) async-start(), calls=%async_computation.3 | async-start | bytes 9191424 | tf_op jit(solution)/shard_map/reduce_scatter | solution.py:643
  16.1 27.1 %collective-permute-start = (bf16[512,1024]{1,0:T(8,128)(2,1)S(1)}, bf16[512,1024]{1,0:T(8,128)(2,1)}, u32[]{:S(2)}, u32[]{:S(2)}) collective-permute-start(bf16[512,1024]{1,0:T(8,128)(2,1)S(1)} %fusion.38), channel_id=1, source_target_pairs={{0,1},{1,0},{2,3},{3,2},{4,5},{5,4},{6,7},{7,6},{8,9},{9,8},{10,11... | collective-permute-start | bytes 3145736 | tf_op jit(solution)/shard_map/ppermute | solution.py:434
  19.2 45.7 %collective-permute-start.1 = (bf16[512,1024]{1,0:T(8,128)(2,1)}, bf16[512,1024]{1,0:T(8,128)(2,1)}, u32[]{:S(2)}, u32[]{:S(2)}) collective-permute-start(bf16[512,1024]{1,0:T(8,128)(2,1)} %param.21), channel_id=1, source_target_pairs={{0,1},{1,0},{2,3},{3,2},{4,5},{5,4},{6,7},{7,6},{8,9},{9,8},{10,11... | collective-permute-start | bytes 3145736 | tf_op jit(solution)/shard_map/ppermute | solution.py:434
  67.0 18.9 %collective-permute-start.2 = (bf16[512,512]{1,0:T(8,128)(2,1)S(1)}, bf16[512,512]{1,0:T(8,128)(2,1)}, u32[]{:S(2)}, u32[]{:S(2)}) collective-permute-start(bf16[512,512]{1,0:T(8,128)(2,1)S(1)} %constant_dynamic-slice_fusion.2), channel_id=1, source_target_pairs={{0,1},{1,0},{2,3},{3,2},{4,5},{5,4},{6,7},{7,6},{8,9},{9,8},{10,11... | collective-permute-start | bytes 1572872 | tf_op jit(solution)/shard_map/ppermute | solution.py:434
  86.9 14.7 %collective-permute-start.3 = (bf16[512,512]{1,0:T(8,128)(2,1)}, bf16[512,512]{1,0:T(8,128)(2,1)}, u32[]{:S(2)}, u32[]{:S(2)}) collective-permute-start(bf16[512,512]{1,0:T(8,128)(2,1)} %get-tuple-element.89), channel_id=1, source_target_pairs={{0,1},{1,0},{2,3},{3,2},{4,5},{5,4},{6,7},{7,6},{8,9},{9,8},{10,11... | collective-permute-start | bytes 1572872 | tf_op jit(solution)/shard_map/ppermute | solution.py:434
  106.8 25.2 %collective-permute-start.5 = (bf16[512,1024]{1,0:T(8,128)(2,1)}, bf16[512,1024]{1,0:T(8,128)(2,1)}, u32[]{:S(2)}, u32[]{:S(2)}) collective-permute-start(bf16[512,1024]{1,0:T(8,128)(2,1)} %multiply_convert_fusion.6), channel_id=1, source_target_pairs={{0,1},{1,0},{2,3},{3,2},{4,5},{5,4},{6,7},{7,6},{8,9},{9,8},{10,11... | collective-permute-start | bytes 3145736 | tf_op jit(solution)/shard_map/ppermute | solution.py:434
  168.8 29.9 %collective-permute-start.6 = (bf16[512,1024]{1,0:T(8,128)(2,1)}, bf16[512,1024]{1,0:T(8,128)(2,1)}, u32[]{:S(2)}, u32[]{:S(2)}) collective-permute-start(bf16[512,1024]{1,0:T(8,128)(2,1)} %fusion.62), channel_id=1, source_target_pairs={{0,1},{1,0},{2,3},{3,2},{4,5},{5,4},{6,7},{7,6},{8,9},{9,8},{10,11... | collective-permute-start | bytes 3145736 | tf_op jit(solution)/shard_map/ppermute | solution.py:434
  211.8 13.9 %collective-permute-start.7 = (bf16[512,512]{1,0:T(8,128)(2,1)S(1)}, bf16[512,512]{1,0:T(8,128)(2,1)S(1)}, u32[]{:S(2)}, u32[]{:S(2)}) collective-permute-start(bf16[512,512]{1,0:T(8,128)(2,1)S(1)} %convolution_convert_fusion.5), channel_id=1, source_target_pairs={{0,1},{1,0},{2,3},{3,2},{4,5},{5,4},{6,7},{7,6},{8,9},{9,8},{10,11... | collective-permute-start | bytes 1572872 | tf_op jit(solution)/shard_map/ppermute | solution.py:434
  225.8 28.1 %collective-permute-start.8 = (bf16[512,1024]{1,0:T(8,128)(2,1)S(1)}, bf16[512,1024]{1,0:T(8,128)(2,1)S(1)}, u32[]{:S(2)}, u32[]{:S(2)}) collective-permute-start(bf16[512,1024]{1,0:T(8,128)(2,1)S(1)} %fusion.59), channel_id=1, source_target_pairs={{0,1},{1,0},{2,3},{3,2},{4,5},{5,4},{6,7},{7,6},{8,9},{9,8},{10,11... | collective-permute-start | bytes 3145736 | tf_op jit(solution)/shard_map/ppermute | solution.py:434
  254.3 9.2 %collective-permute-start.9 = (bf16[8,64,1536]{2,1,0:T(8,128)(2,1)S(1)}, bf16[8,64,1536]{2,1,0:T(8,128)(2,1)S(1)}, u32[]{:S(2)}, u32[]{:S(2)}) collective-permute-start(bf16[8,64,1536]{2,1,0:T(8,128)(2,1)S(1)} %dynamic-slice_bitcast_fusion), channel_id=1, source_target_pairs={{0,2},{2,0},{4,6},{6,4},{8,10},{10,8},{12,14},{14,12},{16,18},{18,... | collective-permute-start | bytes 4718600 | tf_op jit(solution)/shard_map/ppermute | solution.py:443
  261.7 12.8 %collective-permute-start.11 = (bf16[512,512]{1,0:T(8,128)(2,1)S(1)}, bf16[512,512]{1,0:T(8,128)(2,1)S(1)}, u32[]{:S(2)}, u32[]{:S(2)}) collective-permute-start(bf16[512,512]{1,0:T(8,128)(2,1)S(1)} %slice.106), channel_id=1, source_target_pairs={{0,1},{1,0},{2,3},{3,2},{4,5},{5,4},{6,7},{7,6},{8,9},{9,8},{10,11... | collective-permute-start | bytes 1572872 | tf_op jit(solution)/shard_map/ppermute | solution.py:434
  274.6 72.5 %collective-permute-start.12 = (bf16[512,1024]{1,0:T(8,128)(2,1)S(1)}, bf16[512,1024]{1,0:T(8,128)(2,1)S(1)}, u32[]{:S(2)}, u32[]{:S(2)}) collective-permute-start(bf16[512,1024]{1,0:T(8,128)(2,1)S(1)} %slice.88), channel_id=1, source_target_pairs={{0,1},{1,0},{2,3},{3,2},{4,5},{5,4},{6,7},{7,6},{8,9},{9,8},{10,11... | collective-permute-start | bytes 3145736 | tf_op jit(solution)/shard_map/ppermute | solution.py:434
  276.5 29.6 %collective-permute-start.13 = (bf16[2,2,64,768]{3,2,1,0:T(8,128)(2,1)S(1)}, bf16[2,2,64,768]{3,2,1,0:T(8,128)(2,1)S(1)}, u32[]{:S(2)}, u32[]{:S(2)}) collective-permute-start(bf16[2,2,64,768]{3,2,1,0:T(8,128)(2,1)S(1)} %dynamic-slice_bitcast_fusion.2), channel_id=1, source_target_pairs={{0,4},{2,6},{4,0},{6,2},{8,12},{10,14},{12,8},{14,10},{16,20},{18,... | collective-permute-start | bytes 1179656 | tf_op jit(solution)/shard_map/ppermute | solution.py:465
  276.7 31.4 %collective-permute-start.15 = (bf16[2,2,64,768]{3,2,0,1:T(8,128)(2,1)S(1)}, bf16[2,2,64,768]{3,2,0,1:T(8,128)(2,1)S(1)}, u32[]{:S(2)}, u32[]{:S(2)}) collective-permute-start(bf16[2,2,64,768]{3,2,0,1:T(8,128)(2,1)S(1)} %bitcast.116), channel_id=1, source_target_pairs={{0,4},{2,6},{4,0},{6,2},{8,12},{10,14},{12,8},{14,10},{16,20},{18,... | collective-permute-start | bytes 1179656 | tf_op jit(solution)/shard_map/ppermute | solution.py:465
  279.0 26.1 %collective-permute-start.24 = (bf16[2,2,64,512]{3,2,1,0:T(8,128)(2,1)S(1)}, bf16[2,2,64,512]{3,2,1,0:T(8,128)(2,1)S(1)}, u32[]{:S(2)}, u32[]{:S(2)}) collective-permute-start(bf16[2,2,64,512]{3,2,1,0:T(8,128)(2,1)S(1)} %dynamic-slice_bitcast_fusion.3), channel_id=1, source_target_pairs={{0,4},{2,6},{4,0},{6,2},{8,12},{10,14},{12,8},{14,10},{16,20},{18,... | collective-permute-start | bytes 786440 | tf_op jit(solution)/shard_map/ppermute | solution.py:465
  307.0 16.8 %collective-permute-start.14 = (bf16[2,64,768]{2,1,0:T(8,128)(2,1)}, bf16[2,64,768]{2,1,0:T(8,128)(2,1)}, u32[]{:S(2)}, u32[]{:S(2)}) collective-permute-start(bf16[2,64,768]{2,1,0:T(8,128)(2,1)} %dynamic-slice_bitcast_fusion.5), channel_id=1, source_target_pairs={{0,8},{2,10},{4,12},{6,14},{8,0},{10,2},{12,4},{14,6},{16,24},{18,... | collective-permute-start | bytes 589832 | tf_op jit(solution)/shard_map/ppermute | solution.py:465
  308.4 11.0 %collective-permute-start.16 = (bf16[48,1024]{1,0:T(8,128)(2,1)S(1)}, bf16[48,1024]{1,0:T(8,128)(2,1)S(1)}, u32[]{:S(2)}, u32[]{:S(2)}) collective-permute-start(bf16[48,1024]{1,0:T(8,128)(2,1)S(1)} %convert_element_type.344), channel_id=1, source_target_pairs={{0,2},{2,0},{4,6},{6,4},{8,10},{10,8},{12,14},{14,12},{16,18},{18,... | collective-permute-start | bytes 294920 | tf_op jit(solution)/shard_map/ppermute | solution.py:501
  314.4 7.8 %collective-permute-start.21 = (bf16[2,64,768]{2,1,0:T(8,128)(2,1)S(1)}, bf16[2,64,768]{2,1,0:T(8,128)(2,1)S(1)}, u32[]{:S(2)}, u32[]{:S(2)}) collective-permute-start(bf16[2,64,768]{2,1,0:T(8,128)(2,1)S(1)} %dynamic-slice_bitcast_fusion.4), channel_id=1, source_target_pairs={{0,8},{2,10},{4,12},{6,14},{8,0},{10,2},{12,4},{14,6},{16,24},{18,... | collective-permute-start | bytes 589832 | tf_op jit(solution)/shard_map/ppermute | solution.py:465
  319.4 7.0 %collective-permute-start.17 = (bf16[48,1024]{1,0:T(8,128)(2,1)S(1)}, bf16[48,1024]{1,0:T(8,128)(2,1)S(1)}, u32[]{:S(2)}, u32[]{:S(2)}) collective-permute-start(bf16[48,1024]{1,0:T(8,128)(2,1)S(1)} %add_convert_fusion.5), channel_id=1, source_target_pairs={{0,8},{2,10},{4,12},{6,14},{8,0},{10,2},{12,4},{14,6},{16,24},{18,... | collective-permute-start | bytes 294920 | tf_op jit(solution)/shard_map/ppermute | solution.py:501
  322.3 9.4 %collective-permute-start.22 = (bf16[64,768]{1,0:T(8,128)(2,1)S(1)}, bf16[64,768]{1,0:T(8,128)(2,1)S(1)}, u32[]{:S(2)}, u32[]{:S(2)}) collective-permute-start(bf16[64,768]{1,0:T(8,128)(2,1)S(1)} %dynamic-slice_bitcast_fusion.8), channel_id=1, source_target_pairs={{0,16},{2,18},{4,20},{6,22},{8,24},{10,26},{12,28},{14,30},{16,0},... | collective-permute-start | bytes 294920 | tf_op jit(solution)/shard_map/ppermute | solution.py:465
  324.8 8.8 %collective-permute-start.23 = (bf16[64,768]{1,0:T(8,128)(2,1)S(1)}, bf16[64,768]{1,0:T(8,128)(2,1)S(1)}, u32[]{:S(2)}, u32[]{:S(2)}) collective-permute-start(bf16[64,768]{1,0:T(8,128)(2,1)S(1)} %dynamic-slice_bitcast_fusion.7), channel_id=1, source_target_pairs={{0,16},{2,18},{4,20},{6,22},{8,24},{10,26},{12,28},{14,30},{16,0},... | collective-permute-start | bytes 294920 | tf_op jit(solution)/shard_map/ppermute | solution.py:465
  326.4 8.3 %collective-permute-start.18 = (bf16[48,1024]{1,0:T(8,128)(2,1)S(1)}, bf16[48,1024]{1,0:T(8,128)(2,1)S(1)}, u32[]{:S(2)}, u32[]{:S(2)}) collective-permute-start(bf16[48,1024]{1,0:T(8,128)(2,1)S(1)} %add_convert_fusion.4), channel_id=1, source_target_pairs={{0,16},{2,18},{4,20},{6,22},{8,24},{10,26},{12,28},{14,30},{16,0},... | collective-permute-start | bytes 294920 | tf_op jit(solution)/shard_map/ppermute | solution.py:501
  (57 other events, 522.6 us)
Sparse Core Ops, SparseCore 0:
  12.3 53.2 all-gather.2
  67.9 75.0 all-gather.4
  198.9 109.3 reduce-scatter.1
where the time goes:
time: 363 us; the launch traced here: 359 us
  waiting for transfers between devices  146 us (40%)
  matrix products  91.2 us (25%)
  Pallas kernels  31.8 us (9%)
  starting transfers between devices  26.8 us (7%)
  other arithmetic  26.6 us (7%)
  local copies, waits for them, and re-layouts  20.7 us (6%)
  between operations  15.1 us (4%)
    ppermute x11, waiting for transfers between devices, swap_tensor(): return lax.ppermute(values, 'tensor', [(0, 1), (1, 0)])  93.7 us
    dot_general x8, matrix products, nn(): lax.dot_general(left, right, (((1,), (0,)), ((), ())), preferred_element_...  37.7 us
    ppermute x9, waiting for transfers between devices, halving_stage(): arrived = lax.ppermute(sent, 'dp', [(i, i ^ bit) for i in range(count)])  36.2 us
    dot_general x7, matrix products, nt(): lax.dot_general(left, right, (((1,), (1,)), ((), ())), preferred_element_...  27.2 us
    dot_general x4, matrix products, tn(): lax.dot_general(left, right, (((0,), (0,)), ((), ())), preferred_element_...  24.7 us
    pallas_call x1, Pallas kernels, mixer_backward(): pl.pallas_call(functools.partial(backward_kernel, heads), grid_spec=pltpu...  21.3 us
    ppermute x11, starting transfers between devices, swap_tensor(): return lax.ppermute(values, 'tensor', [(0, 1), (1, 0)])  14.1 us
    all_gather x1, waiting for transfers between devices, on_device(): lax.all_gather(jnp.concatenate([feed_gate, feed_up, feed_down], axis=1),...  11 us
  transfers between devices with their start and end apart: 30, of which 18 were waited for; matrix products, arithmetic and copies ran while one was open for 28% of the time, Pallas kernels for 9%

commit v1 on v0

--- a/solution.py
+++ b/solution.py
@@ -660,8 +660,8 @@
     grad_joined, output_grads, fed_back = lax.optimization_barrier(
         (grad_joined, output_grads, fed_back)
     )
-    projected_chip, hidden_last = lax.optimization_barrier(
-        (chip_sum(grad_joined[:, :projected_width]), hidden_own)
+    projected_chip, hidden_last, packed = lax.optimization_barrier(
+        (chip_sum(grad_joined[:, :projected_width]), hidden_own, packed)
     )
     joined_sums = [
         halving_stage(by_chip(piece), 0) for piece in jnp.split(projected_chip, 2, axis=1)
@@ -671,12 +671,12 @@
     joined_back = jnp.concatenate([joined_in, lane_pad(decay_down, 1)], axis=1)
     normed_part = nt(grad_projected, joined_back)
     grad_mixer_gain = jnp.sum(normed_part * normed_all.astype(f32), axis=0) / gain_in
-    normed_part, _ = lax.optimization_barrier((normed_part.astype(bf16), output_back))
+    normed_part = normed_part.astype(bf16)
     fed = nt(hidden_last, feed_down_full) + fed_back.astype(f32)
     output = (middle + fed).astype(bf16)
+    output_back, _ = lax.optimization_barrier((output_back, joined_sums[0]))
     output_total = output_chip[:, :value_width].astype(f32) + output_back.astype(f32)
     joined_sums.append(halving_stage(by_chip(output_total.astype(bf16)), 0))
-    packed, _ = lax.optimization_barrier((packed, joined_sums[0]))
     joined_sums = [halving_stage(held, 1) for held in joined_sums]
     normed_back, _ = lax.optimization_barrier((swap_tensor(normed_part[own:]), joined_sums[1]))
     grad_normed = normed_part[:own].astype(f32) + normed_back.astype(f32)

time: 363 us -> 345 us (0.950)
  waiting for transfers between devices: 146 us -> 129 us
  starting transfers between devices: 26.8 us -> 21.9 us
  local copies, waits for them, and re-layouts: 20.7 us -> 25.2 us
    ppermute x9, waiting for transfers between devices: 36.2 us -> 21 us  [halving_stage(): arrived = lax.ppermute(sent, 'dp', [(i, i ^ bit) for i in range(count)])]
    unnamed x105 -> x115, local copies, waits for them, and re-layouts: 10.9 us -> 11.3 us
  transfers between devices with their start and end apart: 30 -> 30, of which waited for: 18 -> 18; matrix products, arithmetic and copies ran while one was open for 28% -> 30% of each run, Pallas kernels for 9% -> 9%
where the time goes in v1:
time: 345 us; the launch traced here: 340 us
  waiting for transfers between devices  129 us (37%)
  matrix products  91.3 us (26%)
  Pallas kernels  31.8 us (9%)
  other arithmetic  25.9 us (8%)
  local copies, waits for them, and re-layouts  25.2 us (7%)
  starting transfers between devices  21.9 us (6%)
  between operations  15 us (4%)
    ppermute x11, waiting for transfers between devices, swap_tensor(): return lax.ppermute(values, 'tensor', [(0, 1), (1, 0)])  90.7 us
    dot_general x8, matrix products, nn(): lax.dot_general(left, right, (((1,), (0,)), ((), ())), preferred_element_...  37.8 us
    dot_general x7, matrix products, nt(): lax.dot_general(left, right, (((1,), (1,)), ((), ())), preferred_element_...  27.2 us
    dot_general x4, matrix products, tn(): lax.dot_general(left, right, (((0,), (0,)), ((), ())), preferred_element_...  24.7 us
    pallas_call x1, Pallas kernels, mixer_backward(): pl.pallas_call(functools.partial(backward_kernel, heads), grid_spec=pltpu...  21.3 us
    ppermute x9, waiting for transfers between devices, halving_stage(): arrived = lax.ppermute(sent, 'dp', [(i, i ^ bit) for i in range(count)])  21 us
    ppermute x11, starting transfers between devices, swap_tensor(): return lax.ppermute(values, 'tensor', [(0, 1), (1, 0)])  12.3 us
    unnamed x115, local copies, waits for them, and re-layouts  11.3 us
  transfers between devices with their start and end apart: 30, of which 18 were waited for; matrix products, arithmetic and copies ran while one was open for 30% of the time, Pallas kernels for 9%

profile of v1, /device:TPU:0, one launch (start us, length us, event | category | flops | bytes accessed | tf_op | source)
XLA Modules:
  0.0 339.9 jit_solution(12267705784213632010)
XLA Ops:
  20.8 22.5 %collective-permute-done = bf16[512,1024]{1,0:T(8,128)(2,1)} collective-permute-done((bf16[512,1024]{1,0:T(8,128)(2,1)S(1)}, bf16[512,1024]{1,0:T(8,128)(2,1)}, u32[]{:S(2)}, u32[]{:S(2)}) %collective-permute-start) | collective-permute-done | bytes 1048608 | tf_op jit(solution)/shard_map/ppermute | solution.py:434
  46.9 18.0 %collective-permute-done.1 = bf16[512,1024]{1,0:T(8,128)(2,1)} collective-permute-done((bf16[512,1024]{1,0:T(8,128)(2,1)}, bf16[512,1024]{1,0:T(8,128)(2,1)}, u32[]{:S(2)}, u32[]{:S(2)}) %collective-permute-start.1) | collective-permute-done | bytes 1048608 | tf_op jit(solution)/shard_map/ppermute | solution.py:434
  68.5 5.5 %convolution_convert_fusion.2.projected = bf16[1024,1536]{1,0:T(8,128)(2,1)S(1)} fusion(bf16[1024,1024]{1,0:T(8,128)(2,1)S(1)} %pad_maximum_fusion.1.normed, bf16[1024,2048]{1,0:T(8,128)(2,1)} %all-gather.3.cloned.1.call-done), kind=kOutput, calls=%fused_computation.20 | convolution fusion | flops 3222798336 | bytes 8388608 | tf_op jit(solution)/shard_map/dot_general | solution.py:63
  74.1 9.4 %mixer_forward.1 = (bf16[1024,512]{1,0:T(8,128)(2,1)S(1)}, bf16[1024,512]{1,0:T(8,128)(2,1)S(1)}, bf16[16,2,256,128]{3,2,1,0:T(8,128)(2,1)S(1)}) custom-call(s32[17]{0:T(128)S(1)} %pad_add_fusion.scal, bf16[1024,1536]{1,0:T(8,128)(2,1)S(1)} %convolution_convert_fusion.2.projected, f32[1024,256]{1,0:T(8,128)S(1)} %copy-done.2, f32[1024,1]{1,0:T(8,128)S(1)} %copy-done.4, ...), custom_call_target="tpu_custom_call" | custom-call | flops 10000000000 | bytes 15000000 | tf_op jit(solution)/shard_map/mixer_forward/pallas_call | solution.py:324
  89.5 12.0 %collective-permute-done.3 = bf16[512,512]{1,0:T(8,128)(2,1)} collective-permute-done((bf16[512,512]{1,0:T(8,128)(2,1)}, bf16[512,512]{1,0:T(8,128)(2,1)}, u32[]{:S(2)}, u32[]{:S(2)}) %collective-permute-start.3) | collective-permute-done | bytes 524320 | tf_op jit(solution)/shard_map/ppermute | solution.py:434
  108.1 23.8 %collective-permute-done.5 = bf16[512,1024]{1,0:T(8,128)(2,1)} collective-permute-done((bf16[512,1024]{1,0:T(8,128)(2,1)}, bf16[512,1024]{1,0:T(8,128)(2,1)}, u32[]{:S(2)}, u32[]{:S(2)}) %collective-permute-start.5) | collective-permute-done | bytes 1048608 | tf_op jit(solution)/shard_map/ppermute | solution.py:434
  131.9 11.0 %all-gather.5.cloned.1.call-done = bf16[1024,4224]{1,0:T(8,128)(2,1)} async-done(((bf16[64,4224]{1,0:T(8,128)(2,1)}), bf16[1024,4224]{1,0:T(8,128)(2,1)}) %all-gather.5.cloned.1.call-update) | async-done | bytes 8650768 | tf_op jit(solution)/shard_map/all_gather | solution.py:557
  142.9 6.2 %fusion.18 = f32[512,2816]{1,0:T(8,128)S(1)} fusion(bf16[512,1024]{1,0:T(8,128)(2,1)} %collective-permute-done.5, bf16[1024,4224]{1,0:T(8,128)(2,1)} %all-gather.5.cloned.1.call-done), kind=kOutput, calls=%fused_computation.27 | convolution fusion | flops 2952790016 | bytes 12582912 | tf_op jit(solution)/shard_map/dot_general | solution.py:63
  149.2 15.5 %multiply_convert_fusion.5 = (bf16[512,1408]{1,0:T(8,128)(2,1)S(1)}, bf16[512,1408]{1,0:T(8,128)(2,1)S(1)}, bf16[512,1408]{1,0:T(8,128)(2,1)}) fusion(f32[512,2816]{1,0:T(8,128)S(1)} %fusion.18, bf16[512,1024]{1,0:T(8,128)(2,1)} %collective-permute-done.1, bf16[1024,4224]{1,0:T(8,128)(2,1)S(1)} %copy-done.45), kind=kOutput, calls=%fused_computation.51 | convolution fusion | flops 1486487552 | bytes 14024704 | tf_op jit(solution)/shard_map/dot_general | solution.py:63
  164.7 4.1 %fusion.62 = bf16[512,1024]{1,0:T(8,128)(2,1)} fusion(bf16[1024,4224]{1,0:T(8,128)(2,1)S(1)} %copy-done.45, bf16[512,1408]{1,0:T(8,128)(2,1)S(1)} %get-tuple-element.81, bf16[512,1408]{1,0:T(8,128)(2,1)S(1)} %get-tuple-element.80), kind=kOutput, calls=%fused_computation.91 | convolution fusion | flops 2959081472 | bytes 9699328 | tf_op jit(solution)/shard_map/dot_general | solution.py:67
  170.3 4.4 %fusion.14 = f32[512,2816]{1,0:T(8,128)S(1)} fusion(bf16[512,1024]{1,0:T(8,128)(2,1)} %multiply_convert_fusion.6, bf16[1024,4224]{1,0:T(8,128)(2,1)S(1)} %copy-done.45), kind=kOutput, calls=%fused_computation.23 | convolution fusion | flops 2952790016 | bytes 12582912 | tf_op jit(solution)/shard_map/dot_general | solution.py:63
  178.8 10.2 %fusion.9 = bf16[1024,2816]{1,0:T(8,128)(2,1)S(1)} fusion(bf16[512,1408]{1,0:T(8,128)(2,1)} %copy-done.54, bf16[512,1408]{1,0:T(8,128)(2,1)} %copy-done.53, bf16[512,1408]{1,0:T(8,128)(2,1)S(1)} %get-tuple-element.79, bf16[512,1408]{1,0:T(8,128)(2,1)S(1)} %get-tuple-element.78, bf16[512,1024]{1,0:T(8,128)(2,1)} %collective-permute-done.5, ...), kind=kOutput, calls=%fused_computation.11 | convolution fusion | flops 5935726592 | bytes 13631488 | tf_op jit(solution)/shard_map/dot_general | solution.py:71
  189.1 5.5 %convolution_convert_fusion.1 = bf16[1024,1408]{1,0:T(8,128)(2,1)S(1)} fusion(bf16[512,1408]{1,0:T(8,128)(2,1)} %get-tuple-element.57, bf16[512,1408]{1,0:T(8,128)(2,1)S(1)} %get-tuple-element.64, bf16[512,1024]{1,0:T(8,128)(2,1)} %collective-permute-done.1, bf16[512,1024]{1,0:T(8,128)(2,1)} %param.21), kind=kOutput, calls=%fused_computation.19 | convolution fusion | flops 2964193280 | bytes 7864320 | tf_op jit(solution)/shard_map/dot_general | solution.py:71
  194.6 4.2 %pad_maximum_fusion = bf16[1024,4224]{1,0:T(8,128)(2,1)} fusion(bf16[1024,1408]{1,0:T(8,128)(2,1)S(1)} %convolution_convert_fusion.1, bf16[1024,2816]{1,0:T(8,128)(2,1)S(1)} %fusion.9), kind=kLoop, calls=%fused_computation | loop fusion | flops 17301504 | bytes 17301504 | tf_op jit(solution)/shard_map/concatenate | solution.py:636
  198.8 8.4 %multiply_reduce_fusion.1 = (f32[1024]{0:T(1024)S(1)}, f32[512]{0:T(512)S(1)}, f32[512,1024]{1,0:T(8,128)S(1)}) fusion(f32[512,1024]{1,0:T(8,128)} %copy-done.14, f32[512]{0:T(512)S(1)} %get-tuple-element.103, bf16[512,1024]{1,0:T(8,128)(2,1)} %collective-permute-done.6, f32[1024]{0:T(1024)S(1)} %convert_element_type.302, ...), kind=kOutput, calls=%fused_computation.73 | convolution fusion | flops 2962749952 | bytes 13905920 | tf_op jit(solution)/shard_map/dot_general | solution.py:67
  220.9 4.9 %collective-permute-done.7 = bf16[512,512]{1,0:T(8,128)(2,1)S(1)} collective-permute-done((bf16[512,512]{1,0:T(8,128)(2,1)S(1)}, bf16[512,512]{1,0:T(8,128)(2,1)S(1)}, u32[]{:S(2)}, u32[]{:S(2)}) %collective-permute-start.7) | collective-permute-done | bytes 524320 | tf_op jit(solution)/shard_map/ppermute | solution.py:434
  226.2 21.3 %mixer_backward.1 = (bf16[1024,1664]{1,0:T(8,128)(2,1)}, f32[48,1024]{1,0:T(8,128)S(1)}) custom-call(s32[17]{0:T(128)S(1)} %pad_add_fusion.scal, bf16[1024,1536]{1,0:T(8,128)(2,1)S(1)} %copy-done.9, f32[1024,256]{1,0:T(8,128)S(1)} %copy-done.3, f32[1024,1]{1,0:T(8,128)S(1)} %copy-done.5, f32[1,256]{1,0:T(1,128)S(1)} %bitcast.100, ...), custom_call_target="tpu_custom_call" | custom-call | flops 24999999488 | bytes 20000000 | tf_op jit(solution)/shard_map/mixer_backward/pallas_call | solution.py:369
  247.6 6.4 %convolution_convert_fusion = bf16[1024,1664]{1,0:T(8,128)(2,1)S(1)} fusion(bf16[1024,1024]{1,0:T(8,128)(2,1)S(1)} %pad_maximum_fusion.1.normed, bf16[1024,1664]{1,0:T(8,128)(2,1)} %get-tuple-element.59), kind=kOutput, calls=%fused_computation.18 | convolution fusion | flops 3491364864 | bytes 8912896 | tf_op jit(solution)/shard_map/dot_general | solution.py:71
  257.5 4.2 %multiply_reduce_fusion = (f32[1024]{0:T(1024)S(1)}, bf16[1024,1024]{1,0:T(8,128)(2,1)S(1)}) fusion(bf16[1024,1024]{1,0:T(8,128)(2,1)S(1)} %pad_maximum_fusion.1.normed, bf16[1024,1664]{1,0:T(8,128)(2,1)S(1)} %copy-done.50, bf16[1024,16]{1,0:T(8,128)(2,1)S(1)} %copy.57, bf16[1024,1536]{1,0:T(8,128)(2,1)S(1)} %slice-done), kind=kOutput, calls=%fused_computation.12 | convolution fusion | flops 3504077824 | bytes 10784768 | tf_op jit(solution)/shard_map/dot_general | solution.py:67
  280.2 4.4 %collective-permute-done.15 = bf16[48,1024]{1,0:T(8,128)(2,1)S(1)} collective-permute-done((bf16[48,1024]{1,0:T(8,128)(2,1)S(1)}, bf16[48,1024]{1,0:T(8,128)(2,1)S(1)}, u32[]{:S(2)}, u32[]{:S(2)}) %collective-permute-start.15) | collective-permute-done | bytes 98336 | tf_op jit(solution)/shard_map/ppermute | solution.py:501
  286.5 4.9 %collective-permute-done.18 = bf16[2,2,64,768]{3,2,0,1:T(8,128)(2,1)S(1)} collective-permute-done((bf16[2,2,64,768]{3,2,0,1:T(8,128)(2,1)S(1)}, bf16[2,2,64,768]{3,2,0,1:T(8,128)(2,1)S(1)}, u32[]{:S(2)}, u32[]{:S(2)}) %collective-permute-start.18) | collective-permute-done | bytes 393248 | tf_op jit(solution)/shard_map/ppermute | solution.py:465
  291.6 6.7 %collective-permute-done.23 = bf16[512,512]{1,0:T(8,128)(2,1)S(1)} collective-permute-done((bf16[512,512]{1,0:T(8,128)(2,1)}, bf16[512,512]{1,0:T(8,128)(2,1)S(1)}, u32[]{:S(2)}, u32[]{:S(2)}) %collective-permute-start.23) | collective-permute-done | bytes 524320 | tf_op jit(solution)/shard_map/ppermute | solution.py:434
  306.4 7.7 %collective-permute-done.19 = bf16[2,64,768]{2,1,0:T(8,128)(2,1)S(1)} collective-permute-done((bf16[2,64,768]{2,1,0:T(8,128)(2,1)S(1)}, bf16[2,64,768]{2,1,0:T(8,128)(2,1)S(1)}, u32[]{:S(2)}, u32[]{:S(2)}) %collective-permute-start.19) | collective-permute-done | bytes 196640 | tf_op jit(solution)/shard_map/ppermute | solution.py:465
  326.3 4.2 %collective-permute-done.26 = bf16[64,512]{1,0:T(8,128)(2,1)S(1)} collective-permute-done((bf16[64,512]{1,0:T(8,128)(2,1)S(1)}, bf16[64,512]{1,0:T(8,128)(2,1)S(1)}, u32[]{:S(2)}, u32[]{:S(2)}) %collective-permute-start.26) | collective-permute-done | bytes 65568 | tf_op jit(solution)/shard_map/ppermute | solution.py:465
  (260 shorter events, 99.3 us)
Async XLA Ops:
  7.2 58.3 %all-gather.3.cloned.1.call-start = ((), (), s32[]{:S(2)}) async-start(), calls=%async_computation.1 | async-start | bytes 4456448 | tf_op jit(solution)/shard_map/all_gather | solution.py:549
  12.2 130.8 %all-gather.5.cloned.1.call-start = ((), (), s32[]{:S(2)}) async-start(), calls=%async_computation.2 | async-start | bytes 9191424 | tf_op jit(solution)/shard_map/all_gather | solution.py:557
  14.2 316.9 %reduce-scatter.2.cloned.1.call-start = ((), (), s32[]{:S(2)}) async-start(), calls=%async_computation.3 | async-start | bytes 9191424 | tf_op jit(solution)/shard_map/reduce_scatter | solution.py:643
  16.1 27.1 %collective-permute-start = (bf16[512,1024]{1,0:T(8,128)(2,1)S(1)}, bf16[512,1024]{1,0:T(8,128)(2,1)}, u32[]{:S(2)}, u32[]{:S(2)}) collective-permute-start(bf16[512,1024]{1,0:T(8,128)(2,1)S(1)} %fusion.38), channel_id=1, source_target_pairs={{0,1},{1,0},{2,3},{3,2},{4,5},{5,4},{6,7},{7,6},{8,9},{9,8},{10,11... | collective-permute-start | bytes 3145736 | tf_op jit(solution)/shard_map/ppermute | solution.py:434
  19.2 45.7 %collective-permute-start.1 = (bf16[512,1024]{1,0:T(8,128)(2,1)}, bf16[512,1024]{1,0:T(8,128)(2,1)}, u32[]{:S(2)}, u32[]{:S(2)}) collective-permute-start(bf16[512,1024]{1,0:T(8,128)(2,1)} %param.21), channel_id=1, source_target_pairs={{0,1},{1,0},{2,3},{3,2},{4,5},{5,4},{6,7},{7,6},{8,9},{9,8},{10,11... | collective-permute-start | bytes 3145736 | tf_op jit(solution)/shard_map/ppermute | solution.py:434
  67.0 18.8 %collective-permute-start.2 = (bf16[512,512]{1,0:T(8,128)(2,1)S(1)}, bf16[512,512]{1,0:T(8,128)(2,1)}, u32[]{:S(2)}, u32[]{:S(2)}) collective-permute-start(bf16[512,512]{1,0:T(8,128)(2,1)S(1)} %constant_dynamic-slice_fusion.2), channel_id=1, source_target_pairs={{0,1},{1,0},{2,3},{3,2},{4,5},{5,4},{6,7},{7,6},{8,9},{9,8},{10,11... | collective-permute-start | bytes 1572872 | tf_op jit(solution)/shard_map/ppermute | solution.py:434
  86.8 14.7 %collective-permute-start.3 = (bf16[512,512]{1,0:T(8,128)(2,1)}, bf16[512,512]{1,0:T(8,128)(2,1)}, u32[]{:S(2)}, u32[]{:S(2)}) collective-permute-start(bf16[512,512]{1,0:T(8,128)(2,1)} %get-tuple-element.89), channel_id=1, source_target_pairs={{0,1},{1,0},{2,3},{3,2},{4,5},{5,4},{6,7},{7,6},{8,9},{9,8},{10,11... | collective-permute-start | bytes 1572872 | tf_op jit(solution)/shard_map/ppermute | solution.py:434
  106.7 25.2 %collective-permute-start.5 = (bf16[512,1024]{1,0:T(8,128)(2,1)}, bf16[512,1024]{1,0:T(8,128)(2,1)}, u32[]{:S(2)}, u32[]{:S(2)}) collective-permute-start(bf16[512,1024]{1,0:T(8,128)(2,1)} %multiply_convert_fusion.6), channel_id=1, source_target_pairs={{0,1},{1,0},{2,3},{3,2},{4,5},{5,4},{6,7},{7,6},{8,9},{9,8},{10,11... | collective-permute-start | bytes 3145736 | tf_op jit(solution)/shard_map/ppermute | solution.py:434
  168.8 30.0 %collective-permute-start.6 = (bf16[512,1024]{1,0:T(8,128)(2,1)}, bf16[512,1024]{1,0:T(8,128)(2,1)}, u32[]{:S(2)}, u32[]{:S(2)}) collective-permute-start(bf16[512,1024]{1,0:T(8,128)(2,1)} %fusion.62), channel_id=1, source_target_pairs={{0,1},{1,0},{2,3},{3,2},{4,5},{5,4},{6,7},{7,6},{8,9},{9,8},{10,11... | collective-permute-start | bytes 3145736 | tf_op jit(solution)/shard_map/ppermute | solution.py:434
  211.9 13.9 %collective-permute-start.7 = (bf16[512,512]{1,0:T(8,128)(2,1)S(1)}, bf16[512,512]{1,0:T(8,128)(2,1)S(1)}, u32[]{:S(2)}, u32[]{:S(2)}) collective-permute-start(bf16[512,512]{1,0:T(8,128)(2,1)S(1)} %convolution_convert_fusion.5), channel_id=1, source_target_pairs={{0,1},{1,0},{2,3},{3,2},{4,5},{5,4},{6,7},{7,6},{8,9},{9,8},{10,11... | collective-permute-start | bytes 1572872 | tf_op jit(solution)/shard_map/ppermute | solution.py:434
  225.9 28.1 %collective-permute-start.8 = (bf16[512,1024]{1,0:T(8,128)(2,1)S(1)}, bf16[512,1024]{1,0:T(8,128)(2,1)S(1)}, u32[]{:S(2)}, u32[]{:S(2)}) collective-permute-start(bf16[512,1024]{1,0:T(8,128)(2,1)S(1)} %fusion.59), channel_id=1, source_target_pairs={{0,1},{1,0},{2,3},{3,2},{4,5},{5,4},{6,7},{7,6},{8,9},{9,8},{10,11... | collective-permute-start | bytes 3145736 | tf_op jit(solution)/shard_map/ppermute | solution.py:434
  255.2 11.1 %collective-permute-start.9 = (bf16[8,64,1536]{2,1,0:T(8,128)(2,1)S(1)}, bf16[8,64,1536]{2,1,0:T(8,128)(2,1)S(1)}, u32[]{:S(2)}, u32[]{:S(2)}) collective-permute-start(bf16[8,64,1536]{2,1,0:T(8,128)(2,1)S(1)} %dynamic-slice_bitcast_fusion), channel_id=1, source_target_pairs={{0,2},{2,0},{4,6},{6,4},{8,10},{10,8},{12,14},{14,12},{16,18},{18,... | collective-permute-start | bytes 4718600 | tf_op jit(solution)/shard_map/ppermute | solution.py:443
  255.3 9.4 %collective-permute-start.22 = (bf16[8,64,1024]{2,1,0:T(8,128)(2,1)S(1)}, bf16[8,64,1024]{2,1,0:T(8,128)(2,1)S(1)}, u32[]{:S(2)}, u32[]{:S(2)}) collective-permute-start(bf16[8,64,1024]{2,1,0:T(8,128)(2,1)S(1)} %dynamic-slice_bitcast_fusion.1), channel_id=1, source_target_pairs={{0,2},{2,0},{4,6},{6,4},{8,10},{10,8},{12,14},{14,12},{16,18},{18,... | collective-permute-start | bytes 3145736 | tf_op jit(solution)/shard_map/ppermute | solution.py:443
  262.9 43.4 %collective-permute-start.10 = (bf16[512,1024]{1,0:T(8,128)(2,1)}, bf16[512,1024]{1,0:T(8,128)(2,1)S(1)}, u32[]{:S(2)}, u32[]{:S(2)}) collective-permute-start(bf16[512,1024]{1,0:T(8,128)(2,1)} %slice.107), channel_id=1, source_target_pairs={{0,1},{1,0},{2,3},{3,2},{4,5},{5,4},{6,7},{7,6},{8,9},{9,8},{10,11... | collective-permute-start | bytes 3145736 | tf_op jit(solution)/shard_map/ppermute | solution.py:434
  266.0 32.4 %collective-permute-start.23 = (bf16[512,512]{1,0:T(8,128)(2,1)}, bf16[512,512]{1,0:T(8,128)(2,1)S(1)}, u32[]{:S(2)}, u32[]{:S(2)}) collective-permute-start(bf16[512,512]{1,0:T(8,128)(2,1)} %slice.113), channel_id=1, source_target_pairs={{0,1},{1,0},{2,3},{3,2},{4,5},{5,4},{6,7},{7,6},{8,9},{9,8},{10,11... | collective-permute-start | bytes 1572872 | tf_op jit(solution)/shard_map/ppermute | solution.py:434
  268.5 16.7 %collective-permute-start.11 = (bf16[2,2,64,768]{3,2,1,0:T(8,128)(2,1)}, bf16[2,2,64,768]{3,2,1,0:T(8,128)(2,1)}, u32[]{:S(2)}, u32[]{:S(2)}) collective-permute-start(bf16[2,2,64,768]{3,2,1,0:T(8,128)(2,1)} %dynamic-slice_bitcast_fusion.2), channel_id=1, source_target_pairs={{0,4},{2,6},{4,0},{6,2},{8,12},{10,14},{12,8},{14,10},{16,20},{18,... | collective-permute-start | bytes 1179656 | tf_op jit(solution)/shard_map/ppermute | solution.py:465
  270.5 20.9 %collective-permute-start.18 = (bf16[2,2,64,768]{3,2,0,1:T(8,128)(2,1)S(1)}, bf16[2,2,64,768]{3,2,0,1:T(8,128)(2,1)S(1)}, u32[]{:S(2)}, u32[]{:S(2)}) collective-permute-start(bf16[2,2,64,768]{3,2,0,1:T(8,128)(2,1)S(1)} %bitcast.116), channel_id=1, source_target_pairs={{0,4},{2,6},{4,0},{6,2},{8,12},{10,14},{12,8},{14,10},{16,20},{18,... | collective-permute-start | bytes 1179656 | tf_op jit(solution)/shard_map/ppermute | solution.py:465
  277.1 7.5 %collective-permute-start.15 = (bf16[48,1024]{1,0:T(8,128)(2,1)S(1)}, bf16[48,1024]{1,0:T(8,128)(2,1)S(1)}, u32[]{:S(2)}, u32[]{:S(2)}) collective-permute-start(bf16[48,1024]{1,0:T(8,128)(2,1)S(1)} %add_convert_fusion.4), channel_id=1, source_target_pairs={{0,16},{2,18},{4,20},{6,22},{8,24},{10,26},{12,28},{14,30},{16,0},... | collective-permute-start | bytes 294920 | tf_op jit(solution)/shard_map/ppermute | solution.py:501
  284.6 13.9 %collective-permute-start.16 = (bf16[48,1024]{1,0:T(8,128)(2,1)S(1)}, bf16[48,1024]{1,0:T(8,128)(2,1)S(1)}, u32[]{:S(2)}, u32[]{:S(2)}) collective-permute-start(bf16[48,1024]{1,0:T(8,128)(2,1)S(1)} %add_convert_fusion.3), channel_id=1, source_target_pairs={{0,4},{2,6},{4,0},{6,2},{8,12},{10,14},{12,8},{14,10},{16,20},{18,... | collective-permute-start | bytes 294920 | tf_op jit(solution)/shard_map/ppermute | solution.py:501
  286.4 19.9 %collective-permute-start.12 = (bf16[2,64,768]{2,1,0:T(8,128)(2,1)S(1)}, bf16[2,64,768]{2,1,0:T(8,128)(2,1)S(1)}, u32[]{:S(2)}, u32[]{:S(2)}) collective-permute-start(bf16[2,64,768]{2,1,0:T(8,128)(2,1)S(1)} %dynamic-slice_bitcast_fusion.5), channel_id=1, source_target_pairs={{0,8},{2,10},{4,12},{6,14},{8,0},{10,2},{12,4},{14,6},{16,24},{18,... | collective-permute-start | bytes 589832 | tf_op jit(solution)/shard_map/ppermute | solution.py:465
  291.5 22.5 %collective-permute-start.19 = (bf16[2,64,768]{2,1,0:T(8,128)(2,1)S(1)}, bf16[2,64,768]{2,1,0:T(8,128)(2,1)S(1)}, u32[]{:S(2)}, u32[]{:S(2)}) collective-permute-start(bf16[2,64,768]{2,1,0:T(8,128)(2,1)S(1)} %dynamic-slice_bitcast_fusion.4), channel_id=1, source_target_pairs={{0,8},{2,10},{4,12},{6,14},{8,0},{10,2},{12,4},{14,6},{16,24},{18,... | collective-permute-start | bytes 589832 | tf_op jit(solution)/shard_map/ppermute | solution.py:465
  300.4 19.5 %collective-permute-start.24 = (bf16[2,2,64,512]{3,2,1,0:T(8,128)(2,1)S(1)}, bf16[2,2,64,512]{3,2,1,0:T(8,128)(2,1)S(1)}, u32[]{:S(2)}, u32[]{:S(2)}) collective-permute-start(bf16[2,2,64,512]{3,2,1,0:T(8,128)(2,1)S(1)} %dynamic-slice_bitcast_fusion.3), channel_id=1, source_target_pairs={{0,4},{2,6},{4,0},{6,2},{8,12},{10,14},{12,8},{14,10},{16,20},{18,... | collective-permute-start | bytes 786440 | tf_op jit(solution)/shard_map/ppermute | solution.py:465
  314.2 7.6 %collective-permute-start.20 = (bf16[64,768]{1,0:T(8,128)(2,1)S(1)}, bf16[64,768]{1,0:T(8,128)(2,1)S(1)}, u32[]{:S(2)}, u32[]{:S(2)}) collective-permute-start(bf16[64,768]{1,0:T(8,128)(2,1)S(1)} %dynamic-slice_bitcast_fusion.8), channel_id=1, source_target_pairs={{0,16},{2,18},{4,20},{6,22},{8,24},{10,26},{12,28},{14,30},{16,0},... | collective-permute-start | bytes 294920 | tf_op jit(solution)/shard_map/ppermute | solution.py:465
  314.3 9.1 %collective-permute-start.21 = (bf16[64,768]{1,0:T(8,128)(2,1)S(1)}, bf16[64,768]{1,0:T(8,128)(2,1)S(1)}, u32[]{:S(2)}, u32[]{:S(2)}) collective-permute-start(bf16[64,768]{1,0:T(8,128)(2,1)S(1)} %dynamic-slice_bitcast_fusion.7), channel_id=1, source_target_pairs={{0,16},{2,18},{4,20},{6,22},{8,24},{10,26},{12,28},{14,30},{16,0},... | collective-permute-start | bytes 294920 | tf_op jit(solution)/shard_map/ppermute | solution.py:465
  (62 other events, 518.5 us)
Sparse Core Ops, SparseCore 0:
  12.3 53.2 all-gather.2
  67.9 75.0 all-gather.4
  198.9 116.1 reduce-scatter.1
